TPU v7x, 32 devices: a whole 2x2x4 slice. The times are simulated.
32 devices in a mesh: queue: 16 (over z, x, core), mp: 2 (over y).
Axes of the slice: x: 2, y: 2, z: 4, core: 2. Of those that a mesh axis runs over, the one named last changes fastest.
Arguments:
- speech: bfloat16 [3072, 1024], P(('queue', 'mp')), may hold values from -6 to 6
- weight: bfloat16 [1024, 1024], P(None, 'mp'), may hold values from -0.1875 to 0.1875
- norm_gain: float32 [1024], replicated, may hold values from 0.1 to 1.9
- queue_keys: bfloat16 [12288, 1024], P('queue'), may hold values from -96 to 96
- new_keys: bfloat16 [768, 1024], replicated, may hold values from -6 to 6
- pointer: int32 [1], replicated, may hold values from 0 to 12287
- positives: int32 [3072], P(('queue', 'mp')), may hold values from 0 to 12287
Outputs:
- loss: float32 [3072], P(('queue', 'mp'))
- grad_speech: bfloat16 [3072, 1024], P(('queue', 'mp'))
- queue_next: bfloat16 [12288, 1024], P('queue')
All inputs are finite; a program needn't handle non-finite values.
Results may differ from a plain program's by a relative error of at most 0.022.
The roundings to bfloat16 on the way count: a program that leaves them out, or rounds other values in their place, can miss the bound.
Values may be sent and summed in bfloat16 or wider, within the bound.
A program may use at most 128 MiB of HBM per device.

v0:
```python
import math

import jax
import jax.numpy as jnp
from jax import lax
from jax.sharding import PartitionSpec as P


def score_rows(all_queries, columns, key_rows, factor):
    total_rows = all_queries.shape[0]
    block_rows = math.gcd(total_rows, 512)
    block_count = total_rows // block_rows

    def score_block(pieces):
        query_block, column_block = pieces
        scores = (
            lax.dot_general(
                query_block, key_rows, (((1,), (1,)), ((), ())), preferred_element_type=jnp.float32
            )
            * factor
        )
        row_peak = jnp.max(scores, axis=1)
        row_total = jnp.sum(jnp.exp(scores - row_peak[:, None]), axis=1)
        is_positive = lax.broadcasted_iota(jnp.int32, scores.shape, 1) == column_block[:, None]
        row_positive = jnp.sum(jnp.where(is_positive, scores, 0.0), axis=1)
        return (scores, row_peak, row_total, row_positive)

    scores, row_peak, row_total, row_positive = lax.map(
        score_block,
        (
            all_queries.reshape(block_count, block_rows, -1),
            columns.reshape(block_count, block_rows),
        ),
    )
    return (
        scores.reshape(total_rows, -1),
        row_peak.reshape(-1),
        row_total.reshape(-1),
        row_positive.reshape(-1),
    )


def weighted_rows(scores, log_total, columns, key_rows):
    total_rows = scores.shape[0]
    block_rows = math.gcd(total_rows, 512)
    block_count = total_rows // block_rows

    def weight_block(pieces):
        score_block, total_block, column_block = pieces
        is_positive = lax.broadcasted_iota(jnp.int32, score_block.shape, 1) == column_block[:, None]
        weights = (
            jnp.exp(score_block - total_block[:, None]) - is_positive.astype(jnp.float32)
        ).astype(jnp.bfloat16)
        return jnp.dot(weights, key_rows, preferred_element_type=jnp.float32)

    result = lax.map(
        weight_block,
        (
            scores.reshape(block_count, block_rows, -1),
            log_total.reshape(block_count, block_rows),
            columns.reshape(block_count, block_rows),
        ),
    )
    return result.reshape(total_rows, key_rows.shape[1])


def shards(speech, weight, norm_gain, queue_keys, new_keys, pointer, positives):
    full_weight = lax.all_gather(weight, "mp", axis=1, tiled=True)
    hidden = jnp.dot(speech, full_weight, preferred_element_type=jnp.float32)
    inverse_rms = lax.rsqrt(jnp.mean(hidden * hidden, axis=1, keepdims=True) + 1e-06)
    queries = (hidden * inverse_rms * norm_gain).astype(jnp.bfloat16)
    all_queries, all_positives = (
        lax.all_gather(queries, "queue", axis=0, tiled=True),
        lax.all_gather(positives, "queue", axis=0, tiled=True),
    )
    key_count = queue_keys.shape[0]
    own_rows = speech.shape[0]
    width = queue_keys.shape[1]
    queue_index = lax.axis_index("queue")
    columns = all_positives - queue_index * key_count
    factor = 2.0 / math.sqrt(width)
    scores, row_peak, row_total, row_positive = score_rows(all_queries, columns, queue_keys, factor)
    global_peak = lax.pmax(row_peak, "queue")
    row_total, row_positive = lax.psum(
        (row_total * jnp.exp(row_peak - global_peak), row_positive), "queue"
    )
    row_peak = global_peak
    log_total = row_peak + jnp.log(row_total)
    losses = log_total - row_positive
    own_start = queue_index * own_rows
    loss_rows = lax.dynamic_slice_in_dim(losses, own_start, own_rows, 0)
    key_grad = lax.psum_scatter(
        weighted_rows(scores, log_total, columns, queue_keys).astype(jnp.bfloat16),
        "queue",
        scatter_dimension=0,
        tiled=True,
    ).astype(jnp.float32)
    key_grad = key_grad * (16.0 * factor)
    scaled = norm_gain * key_grad
    cubed = inverse_rms * inverse_rms * inverse_rms
    hidden_grad = (
        inverse_rms * scaled
        - hidden * cubed * jnp.sum(scaled * hidden, axis=1, keepdims=True) / width
    ).astype(jnp.bfloat16)
    grad_speech = lax.dot_general(
        hidden_grad, full_weight, (((1,), (1,)), ((), ())), preferred_element_type=jnp.float32
    ).astype(jnp.bfloat16)
    queue_length = key_count * lax.axis_size("queue")
    new_count = new_keys.shape[0]
    row_ids = queue_index * key_count + lax.broadcasted_iota(jnp.int32, (key_count,), 0)
    offsets = (row_ids - pointer[0]) % queue_length
    replaced = offsets < new_count
    taken = jnp.take(new_keys, jnp.minimum(offsets, new_count - 1), axis=0)
    queue_next = jnp.where(replaced[:, None], taken, queue_keys)
    return (loss_rows, grad_speech, queue_next)


def solution(mesh):
    return jax.shard_map(
        shards,
        mesh=mesh,
        in_specs=(
            P(("queue", "mp"), None),
            P(None, "mp"),
            P(),
            P("queue", None),
            P(),
            P(),
            P(("queue", "mp")),
        ),
        out_specs=(P(("queue", "mp")), P(("queue", "mp"), None), P("queue", None)),
        check_vma=False,
    )
```

profile of v0, /device:TPU:0, one launch (start us, length us, event | category | flops | bytes accessed | tf_op | source)
XLA Modules:
  0.0 302.8 jit_solution(16056536787877223225)
XLA Ops:
  7.2 0.0 copy-start
  7.2 0.0 all-gather.3.cloned.1.call-start
  7.2 0.7 all-gather.3.cloned.1.call-update
  7.9 0.0 copy-start.2
  7.9 0.0 copy-start.5
  7.9 0.0 copy-start.4
  7.9 0.0 all-gather.5.cloned.1.call-start
  8.0 37.4 %all-gather.3.cloned.1.call-done = bf16[1024,1024]{1,0:T(8,128)(2,1)} async-done(((bf16[1024,512]{1,0:T(8,128)(2,1)}), bf16[1024,1024]{1,0:T(8,128)(2,1)}) %all-gather.3.cloned.1.call-update) | async-done | bytes 2097168 | tf_op jit(solution)/shard_map/all_gather | solution.py:68
  45.4 2.3 multiply_reduce_fusion.1
  47.7 0.6 multiply_multiply_fusion
  48.3 0.0 copy-done.2
  48.3 0.8 multiply_convert_fusion
  49.1 0.0 all-gather.5.cloned.1.call-update
  49.1 0.0 reduce-scatter.2.cloned.1.call-start
  49.2 0.0 copy-done.5
  49.2 0.6 dynamic-slice
  50.5 0.0 copy-done.3
  50.5 0.0 copy-done.4
  50.5 0.3 dynamic-update-slice
  50.8 12.3 %all-reduce = s32[1536]{0:T(1024)S(1)} all-reduce(s32[1536]{0:T(1024)S(1)} %dynamic-update-slice), channel_id=1, replica_groups=mesh['queue'=16,'mp'=2] {'queue'}, use_global_device_ids=true, to_apply=%add | all-reduce | flops 1536 | bytes 12288
  63.1 0.6 reshape.99
  63.7 30.8 %all-gather.5.cloned.1.call-done = bf16[1536,1024]{1,0:T(8,128)(2,1)} async-done(((bf16[96,1024]{1,0:T(8,128)(2,1)}), bf16[1536,1024]{1,0:T(8,128)(2,1)}) %all-gather.5.cloned.1.call-update) | async-done | bytes 3145744 | tf_op jit(solution)/shard_map/all_gather | solution.py:73
  94.5 28.0 %while.26 = (s32[]{:T(128)}, f32[3,512,768]{2,1,0:T(8,128)}, f32[3,512]{1,0:T(4,128)}, f32[3,512]{1,0:T(4,128)}, f32[3,512]{1,0:T(4,128)}, /*index=5*/bf16[3,512...) while((s32[]{:T(128)}, f32[3,512,768]{2,1,0:T(8,128)}, ...), condition=%wide.region_5.6_spmd, body=%wide.region_1.5_spmd.sunk | while | flops 808057344 | bytes 8940673 | solution.py:28
  94.5 3.9 %bitcast_dynamic-update-slice_fusion.4 = (f32[3,512,768]{2,1,0:T(8,128)}, f32[512,768]{1,0:T(8,128)S(1)}) fusion(f32[3,512,768]{2,1,0:T(8,128)} %get-tuple-element.231, s32[]{:T(128)} %get-tuple-element.230, bf16[768,1024]{1,0:T(8,128)(2,1)} %get-tuple-element.247, bf16[3,512,1024]{2,1,0:T(8,128)(2,1)} %get-tuple-element.246), kind=kOutput, calls=%fused_computation.1.clone.1 | convolution fusion | flops 805699584 | bytes 5768192 | tf_op jit(solution)/shard_map/while/body/eval_jaxpr/dot_general | solution.py:17
  98.4 0.2 reduce_max.10
  98.5 0.7 constant_dynamic-slice_fusion.6
  99.2 0.6 select_reduce_fusion.2
  99.9 1.3 dynamic_update_slice.28
  101.2 1.3 dynamic_update_slice.27
  102.5 1.3 dynamic_update_slice.26
  103.8 3.9 %bitcast_dynamic-update-slice_fusion.4 = (f32[3,512,768]{2,1,0:T(8,128)}, f32[512,768]{1,0:T(8,128)S(1)}) fusion(f32[3,512,768]{2,1,0:T(8,128)} %get-tuple-element.231, s32[]{:T(128)} %get-tuple-element.230, bf16[768,1024]{1,0:T(8,128)(2,1)} %get-tuple-element.247, bf16[3,512,1024]{2,1,0:T(8,128)(2,1)} %get-tuple-element.246), kind=kOutput, calls=%fused_computation.1.clone.1 | convolution fusion | flops 805699584 | bytes 5768192 | tf_op jit(solution)/shard_map/while/body/eval_jaxpr/dot_general | solution.py:17
  107.7 0.2 reduce_max.10
  107.9 0.7 constant_dynamic-slice_fusion.6
  108.6 0.6 select_reduce_fusion.2
  109.2 1.3 dynamic_update_slice.28
  110.5 1.3 dynamic_update_slice.27
  111.8 1.3 dynamic_update_slice.26
  113.1 3.9 %bitcast_dynamic-update-slice_fusion.4 = (f32[3,512,768]{2,1,0:T(8,128)}, f32[512,768]{1,0:T(8,128)S(1)}) fusion(f32[3,512,768]{2,1,0:T(8,128)} %get-tuple-element.231, s32[]{:T(128)} %get-tuple-element.230, bf16[768,1024]{1,0:T(8,128)(2,1)} %get-tuple-element.247, bf16[3,512,1024]{2,1,0:T(8,128)(2,1)} %get-tuple-element.246), kind=kOutput, calls=%fused_computation.1.clone.1 | convolution fusion | flops 805699584 | bytes 5768192 | tf_op jit(solution)/shard_map/while/body/eval_jaxpr/dot_general | solution.py:17
  117.0 0.2 reduce_max.10
  117.2 0.7 constant_dynamic-slice_fusion.6
  117.9 0.6 select_reduce_fusion.2
  118.5 1.3 dynamic_update_slice.28
  119.8 1.3 dynamic_update_slice.27
  121.1 1.3 dynamic_update_slice.26
  122.5 0.7 reshape.100
  123.2 32.0 %pmax.7 = f32[1536]{0:T(1024)S(1)} all-reduce(f32[1536]{0:T(1024)S(1)} %reshape.100), channel_id=1, replica_groups=mesh['queue'=16,'mp'=2] {'queue'}, use_global_device_ids=true, to_apply=%region_6.7 | all-reduce | flops 1536 | bytes 12288 | tf_op jit(solution)/shard_map/pmax | solution.py:83
  155.1 0.7 reshape.101
  155.8 0.7 reshape.102
  156.5 57.6 %all-reduce.1 = (f32[1536]{0:T(1024)}, f32[1536]{0:T(1024)S(1)}) all-reduce(f32[1536]{0:T(1024)S(1)} %reshape.102, f32[1536]{0:T(1024)S(1)} %exponential_multiply_fusion), channel_id=1, replica_groups=mesh['queue'=16,'mp'=2] {'queue'}, use_global_device_ids=true, to_apply=%region_8.9 | all-reduce | flops 3072 | bytes 24576 | tf_op jit(solution)/shard_map/psum | solution.py:84
  214.2 14.1 %while.27 = (s32[]{:T(128)}, bf16[3,512,1024]{2,1,0:T(8,128)(2,1)}, f32[3,512,768]{2,1,0:T(8,128)}, f32[3,512]{1,0:T(4,128)S(1)}, s32[3,512]{1,0:T(4,128)}, /*index=5*/bf16[768,1024]{1,0:T(8,128)(2,1)}, s32[]{:T(128)}) while((s32[]{:T(128)}, bf16[3,512,1024]{2,1,0:T(8,128)(2,1)}, f32[3,512,768]{2,1,0:T(8,128)}, f32[3,512]{1,0:T(4,128)S(1)}, ...), condition=%wide.region_10.11_spmd, body=%wide.region_9.10_spmd.sunk | while | flops 807272448 | bytes 5256277 | solution.py:56
  214.2 0.7 constant_dynamic-slice_fusion.7
  214.9 4.0 %bitcast_dynamic-update-slice_fusion.5 = bf16[3,512,1024]{2,1,0:T(8,128)(2,1)} fusion(bf16[3,512,1024]{2,1,0:T(8,128)(2,1)} %get-tuple-element.260, s32[]{:T(128)} %get-tuple-element.259, bf16[768,1024]{1,0:T(8,128)(2,1)} %get-tuple-element.271, f32[3,512,768]{2,1,0:T(8,128)} %get-tuple-element.268, s32[512]{0:T(512)S(1)} %bitcast.65, ...), kind=kOutput, calls=%fused_computation.10.clone.1 | convolution fusion | flops 807272448 | bytes 5248000 | tf_op jit(solution)/shard_map/while/body/eval_jaxpr/dot_general | solution.py:54
  218.9 0.7 constant_dynamic-slice_fusion.7
  219.6 4.0 %bitcast_dynamic-update-slice_fusion.5 = bf16[3,512,1024]{2,1,0:T(8,128)(2,1)} fusion(bf16[3,512,1024]{2,1,0:T(8,128)(2,1)} %get-tuple-element.260, s32[]{:T(128)} %get-tuple-element.259, bf16[768,1024]{1,0:T(8,128)(2,1)} %get-tuple-element.271, f32[3,512,768]{2,1,0:T(8,128)} %get-tuple-element.268, s32[512]{0:T(512)S(1)} %bitcast.65, ...), kind=kOutput, calls=%fused_computation.10.clone.1 | convolution fusion | flops 807272448 | bytes 5248000 | tf_op jit(solution)/shard_map/while/body/eval_jaxpr/dot_general | solution.py:54
  223.7 0.7 constant_dynamic-slice_fusion.7
  224.4 4.0 %bitcast_dynamic-update-slice_fusion.5 = bf16[3,512,1024]{2,1,0:T(8,128)(2,1)} fusion(bf16[3,512,1024]{2,1,0:T(8,128)(2,1)} %get-tuple-element.260, s32[]{:T(128)} %get-tuple-element.259, bf16[768,1024]{1,0:T(8,128)(2,1)} %get-tuple-element.271, f32[3,512,768]{2,1,0:T(8,128)} %get-tuple-element.268, s32[512]{0:T(512)S(1)} %bitcast.65, ...), kind=kOutput, calls=%fused_computation.10.clone.1 | convolution fusion | flops 807272448 | bytes 5248000 | tf_op jit(solution)/shard_map/while/body/eval_jaxpr/dot_general | solution.py:54
  228.3 0.0 reduce-scatter.2.cloned.1.call-update
  229.0 0.6 pad_clamp_fusion
  229.7 3.8 %gather_fusion = bf16[768,1024]{1,0:T(8,128)(2,1)} fusion(bf16[768,1024]{1,0:T(8,128)(2,1)S(1)} %copy-done, s32[1024]{0:T(1024)} %pad_clamp_fusion), kind=kCustom, calls=%fused_computation | custom fusion | bytes 3148800 | tf_op jit(solution)/shard_map/jit(_take)/gather | solution.py:113
  233.5 2.9 select_select_fusion
  236.4 1.3 dynamic-slice_subtract_fusion
  237.7 54.3 %reduce-scatter.2.cloned.1.call-done = bf16[96,1024]{1,0:T(8,128)(2,1)} async-done(((bf16[1536,1024]{1,0:T(8,128)(2,1)}), bf16[96,1024]{1,0:T(8,128)(2,1)}) %reduce-scatter.2.cloned.1.call-update) | async-done | bytes 196624 | tf_op jit(solution)/shard_map/reduce_scatter | solution.py:92
  292.0 1.1 multiply_reduce_fusion
  293.1 3.2 %convolution_convert_fusion = bf16[96,1024]{1,0:T(8,128)(2,1)} fusion(bf16[1024,1024]{1,0:T(8,128)(2,1)} %all-gather.3.cloned.1.call-done, f32[96,1024]{1,0:T(8,128)S(1)} %get-tuple-element.122, bf16[96,1024]{1,0:T(8,128)(2,1)} %reduce-scatter.2.cloned.1.call-done, f32[96]{0:T(128)S(1)} %multiply_reduce_fusion, f32[96]{0:T(128)} %get-tuple-element.119, ...), kind=kOutput, calls=%fused_computation.22 | convolution fusion | flops 202211328 | bytes 2888832 | tf_op jit(solution)/shard_map/dot_general | solution.py:105
  (19 shorter events, 0.1 us)
Async XLA Ops:
  7.2 222.5 %copy-start = (bf16[768,1024]{1,0:T(8,128)(2,1)S(1)}, bf16[768,1024]{1,0:T(8,128)(2,1)}, u32[]{:S(2)}) copy-start(bf16[768,1024]{1,0:T(8,128)(2,1)} %param.15) | copy-start | bytes 4718596
  7.2 38.2 %all-gather.3.cloned.1.call-start = ((), (), s32[]{:S(2)}) async-start(), calls=%async_computation.1 | async-start | bytes 3145728 | tf_op jit(solution)/shard_map/all_gather | solution.py:68
  7.9 40.4 %copy-start.2 = (f32[1024]{0:T(1024)S(1)}, f32[1024]{0:T(1024)}, u32[]{:S(2)}) copy-start(f32[1024]{0:T(1024)} %param.13) | copy-start | bytes 12292
  7.9 41.3 %copy-start.5 = (u32[32]{0:T(128)S(1)}, u32[32]{0:T(128)}, u32[]{:S(2)}) copy-start(u32[32]{0:T(128)} %constant.88) | copy-start | bytes 388
  7.9 42.5 %copy-start.4 = (s32[96]{0:T(128)S(1)}, s32[96]{0:T(128)}, u32[]{:S(2)}) copy-start(s32[96]{0:T(128)} %param.17) | copy-start | bytes 1156
  7.9 86.5 %all-gather.5.cloned.1.call-start = ((), (), s32[]{:S(2)}) async-start(), calls=%async_computation.2 | async-start | bytes 3342336 | tf_op jit(solution)/shard_map/all_gather | solution.py:73
  48.3 2.2 copy-start.3
  49.1 242.9 %reduce-scatter.2.cloned.1.call-start = ((), (), s32[]{:S(2)}) async-start(), calls=%async_computation.3 | async-start | bytes 3342336 | tf_op jit(solution)/shard_map/reduce_scatter | solution.py:92
  229.6 3.8 %copy-start.1 = (bf16[768,1024]{1,0:T(8,128)(2,1)S(1)}, bf16[768,1024]{1,0:T(8,128)(2,1)}, u32[]{:S(2)}) copy-start(bf16[768,1024]{1,0:T(8,128)(2,1)} %get-tuple-element.277) | copy-start | bytes 4718596
Sparse Core Ops, SparseCore 0:
  9.6 35.8 all-gather.2
  49.2 45.2 all-gather.4
  228.5 63.4 reduce-scatter.1
where the time goes:
time: 304 us; the launch traced here: 303 us
  waiting for transfers between devices  123 us (40%)
  blocking collectives  102 us (34%)
  matrix products  29.2 us (10%)
  local copies, waits for them, and re-layouts  23.5 us (8%)
  between operations  15.2 us (5%)
  other arithmetic  9.69 us (3%)
    psum x1, blocking collectives, shards(): lax.psum((row_total * jnp.exp(row_peak - global_peak), row_positive), 'qu...  57.6 us
    reduce_scatter x1, waiting for transfers between devices, shards(): lax.psum_scatter(weighted_rows(scores, log_total, columns, queue_keys).as...  54.3 us
    all_gather x1, waiting for transfers between devices, shards(): full_weight = lax.all_gather(weight, 'mp', axis=1, tiled=True)  37.4 us
    pmax x1, blocking collectives, shards(): global_peak = lax.pmax(row_peak, 'queue')  32 us
    all_gather x1, waiting for transfers between devices, shards(): lax.all_gather(queries, 'queue', axis=0, tiled=True)  30.8 us
    unnamed x1, blocking collectives  12.3 us
    dot_general x3, matrix products, weight_block(): return jnp.dot(weights, key_rows, preferred_element_type=jnp.float32)  12 us
    dynamic_update_slice x9, local copies, waits for them, and re-layouts, score_rows(): lax.map(score_block, (all_queries.reshape(block_count, block_rows, -1), c...  11.8 us
  transfers between devices with their start and end apart: 3, of which 3 were waited for; matrix products, arithmetic and copies ran while one was open for 3% of the time, Pallas kernels for 0%

commit v1 on v0

v1 whole, which is shorter than its diff:
```python
import functools
import math

import jax
import jax.numpy as jnp
from jax import lax
from jax.experimental import pallas as pl
from jax.experimental.pallas import tpu as pltpu
from jax.sharding import PartitionSpec as P

MESH = pl.DeviceIdType.MESH
GROUP = 4
WEIGHT_CHUNKS = 4
KEY_CHUNKS = 6
LANES = 128


def column_of(tile, row, count):
    line = jnp.broadcast_to(tile[row : row + 1, :], (LANES, LANES))
    eye = lax.broadcasted_iota(jnp.int32, (LANES, LANES), 0) == lax.broadcasted_iota(
        jnp.int32, (LANES, LANES), 1
    )
    return jnp.sum(jnp.where(eye, line, jnp.zeros_like(line)), axis=1, keepdims=True)[:count]


def row_of(column):
    count = column.shape[0]
    wide = jnp.broadcast_to(column, (count, LANES))
    eye = lax.broadcasted_iota(jnp.int32, (count, LANES), 0) == lax.broadcasted_iota(
        jnp.int32, (count, LANES), 1
    )
    return jnp.sum(jnp.where(eye, wide, jnp.zeros_like(wide)), axis=0, keepdims=True)


def step_kernel(
    n_queue,
    n_mp,
    speech_ref,
    weight_ref,
    gain_ref,
    keys_ref,
    new_ref,
    pointer_ref,
    positives_ref,
    loss_ref,
    grad_ref,
    next_ref,
    keys,
    weights_in,
    queries,
    columns,
    scores,
    probs,
    hidden,
    partial,
    arrived,
    stats,
    local_sem,
    wy_s, wy_r, wx_s, wx_r, wcy_s, wcy_r, wcx_s, wcx_r, wco_s, wco_r,
    kc_s, kc_r, kx_s, kx_r, ky_s, ky_r, kcx_s, kcx_r, kcy_s, kcy_r,
    q_s, q_r, p_s, p_r, st_s, st_r, g_s, g_r,
):
    rows, width = speech_ref.shape
    key_count = keys_ref.shape[0]
    nz = n_queue // GROUP
    me = lax.axis_index("queue")
    mp = lax.axis_index("mp")
    z = me // GROUP
    slot = me % GROUP
    x = slot // 2
    core = slot % 2
    core_peer = me + 1 - 2 * core
    x_peer = me + 2 - 4 * x
    core_slot = slot + 1 - 2 * core
    x_slot = slot + 2 - 4 * x
    diag_slot = core_slot + 2 - 4 * x

    def z_dev(distance):
        return lax.rem(z + distance, nz) * GROUP + slot

    def mp_dev(distance):
        return lax.rem(mp + distance, n_mp)

    def push(src, dst, send, recv, queue, mp_index):
        return pltpu.make_async_remote_copy(
            src_ref=src, dst_ref=dst, send_sem=send, recv_sem=recv,
            device_id=(queue, mp_index), device_id_type=MESH,
        )

    barrier = pltpu.get_barrier_semaphore()
    peers = [(core_peer, mp), (x_peer, mp)]
    peers += [(me, mp_dev(d)) for d in range(1, n_mp)]
    peers += [(z_dev(d), mp) for d in range(1, nz)]
    for peer in peers:
        pl.semaphore_signal(barrier, inc=1, device_id=peer, device_id_type=MESH)

    def key_rows(which, start, count):
        return keys.at[pl.ds(pl.multiple_of(which * key_count + start, 16), count), :]

    own_keys = pltpu.make_async_copy(keys_ref, key_rows(slot, 0, key_count), local_sem.at[0])
    own_weight = pltpu.make_async_copy(weight_ref, weights_in.at[mp], local_sem.at[1])
    own_keys.start()
    own_weight.start()
    pl.semaphore_wait(barrier, len(peers))

    sends = []

    def start(copy):
        copy.start()
        sends.append(copy)

    w_count = width // GROUP // WEIGHT_CHUNKS

    def w_push(dist, quarter, j, shard, sems, queue, mp_index, src=None):
        at = pl.ds(pl.multiple_of(quarter * (width // GROUP) + j * w_count, 16), w_count)
        dst = weights_in.at[shard, at, :]
        return push(
            dst if src is None else src.at[at, :], dst,
            sems[0].at[dist, j], sems[1].at[dist, j], queue, mp_index,
        )

    for j in range(WEIGHT_CHUNKS):
        for d in range(1, n_mp):
            start(w_push(d, slot, j, mp, (wy_s, wy_r), me, mp_dev(d), weight_ref))

    part = key_count // n_mp
    k_count = part // KEY_CHUNKS

    def k_start(shard, j):
        return shard * part + j * k_count

    def key_x(j):
        at = k_start(mp, j)
        return push(
            keys_ref.at[pl.ds(pl.multiple_of(at, 16), k_count), :], key_rows(slot, at, k_count),
            kx_s.at[j], kx_r.at[j], x_peer, mp,
        )

    start(key_x(0))
    start(push(keys_ref, key_rows(slot, 0, key_count), kc_s.at[0], kc_r.at[0], core_peer, mp))

    for j in range(WEIGHT_CHUNKS):
        for d in range(1, n_mp):
            shard = mp_dev(n_mp - d)
            w_push(d, slot, j, shard, (wy_s, wy_r), me, mp).wait_recv()
            start(w_push(d, slot, j, shard, (wx_s, wx_r), x_peer, mp))
            start(w_push(d, slot, j, shard, (wcy_s, wcy_r), core_peer, mp))
    for j in range(1, KEY_CHUNKS):
        start(key_x(j))
    for j in range(WEIGHT_CHUNKS):
        for d in range(1, n_mp):
            shard = mp_dev(n_mp - d)
            w_push(d, x_slot, j, shard, (wx_s, wx_r), x_peer, mp).wait_recv()
            start(w_push(d, x_slot, j, shard, (wcx_s, wcx_r), core_peer, mp))
    own_weight.wait()
    for j in range(WEIGHT_CHUNKS):
        for d in range(1, n_mp):
            shard = mp_dev(n_mp - d)
            w_push(d, core_slot, j, shard, (wcy_s, wcy_r), core_peer, mp).wait_recv()
            w_push(d, diag_slot, j, shard, (wcx_s, wcx_r), core_peer, mp).wait_recv()

    part_width = width // n_mp
    for m in range(n_mp):
        hidden[:, m * part_width : (m + 1) * part_width] = jnp.dot(
            speech_ref[...], weights_in[m], preferred_element_type=jnp.float32
        )
    encoded = hidden[...]
    inverse_rms = lax.rsqrt(jnp.mean(encoded * encoded, axis=1, keepdims=True) + 1e-06)
    own_rows = pl.ds(pl.multiple_of(z * rows, 16), rows)
    queries[own_rows, :] = (encoded * inverse_rms * gain_ref[...]).astype(jnp.bfloat16)
    columns[z] = positives_ref[...]

    def z_rows(index):
        return pl.ds(pl.multiple_of(index * rows, 16), rows)

    def query_push(d, owner, target):
        at = queries.at[z_rows(owner), :]
        return push(at, at, q_s.at[d], q_r.at[d], target, mp)

    def column_push(d, owner, target):
        at = columns.at[owner]
        return push(at, at, p_s.at[d], p_r.at[d], target, mp)

    for d in range(1, nz):
        start(query_push(d, z, z_dev(d)))
        start(column_push(d, z, z_dev(d)))

    def key_forward(shard, j, send, recv, queue, mp_index, which=x_slot):
        at = key_rows(which, k_start(shard, j), k_count)
        return push(at, at, send, recv, queue, mp_index)

    def next_rows(step):
        block = key_count // 3
        at = pl.ds(step * block, block)
        length = key_count * n_queue
        ids = me * key_count + step * block + lax.broadcasted_iota(jnp.int32, (block, 1), 0)
        offsets = ids - pointer_ref[0]
        offsets = jnp.where(offsets < 0, offsets + length, offsets)
        count = new_ref.shape[0]
        chosen = lax.broadcasted_iota(jnp.int32, (block, count), 1) == offsets
        taken = jnp.dot(
            jnp.where(chosen, 1.0, 0.0).astype(jnp.bfloat16), new_ref[...],
            preferred_element_type=jnp.float32,
        )
        held = keys[pl.ds(pl.multiple_of(slot * key_count + step * block, 16), block), :]
        next_ref[at, :] = jnp.where(offsets < count, taken, held.astype(jnp.float32)).astype(
            jnp.bfloat16
        )

    own_keys.wait()
    for step in range(3):
        next_rows(step)

    for j in range(KEY_CHUNKS):
        key_forward(mp, j, kx_s.at[j], kx_r.at[j], x_peer, mp).wait_recv()
        for d in range(1, n_mp):
            start(key_forward(mp, j, ky_s.at[d, j], ky_r.at[d, j], me, mp_dev(d)))
        start(key_forward(mp, j, kcx_s.at[j], kcx_r.at[j], core_peer, mp))
    for j in range(KEY_CHUNKS):
        for d in range(1, n_mp):
            shard = mp_dev(n_mp - d)
            key_forward(shard, j, ky_s.at[d, j], ky_r.at[d, j], me, mp).wait_recv()
            start(key_forward(shard, j, kcy_s.at[d, j], kcy_r.at[d, j], core_peer, mp))
    push(
        keys_ref, key_rows(core_slot, 0, key_count), kc_s.at[0], kc_r.at[0], core_peer, mp
    ).wait_recv()
    for j in range(KEY_CHUNKS):
        key_forward(mp, j, kcx_s.at[j], kcx_r.at[j], core_peer, mp, diag_slot).wait_recv()
        for d in range(1, n_mp):
            shard = mp_dev(n_mp - d)
            key_forward(
                shard, j, kcy_s.at[d, j], kcy_r.at[d, j], core_peer, mp, diag_slot
            ).wait_recv()

    for d in range(1, nz):
        source = lax.rem(z + nz - d, nz)
        query_push(d, source, me).wait_recv()
        column_push(d, source, me).wait_recv()

    factor = 2.0 / math.sqrt(width)
    total_rows = nz * rows
    total_keys = GROUP * key_count
    block = 256
    column = jnp.concatenate(
        [column_of(columns[i], 0, rows) for i in range(nz)], axis=0
    ) - z * total_keys

    def is_positive(step):
        ids = step * block + lax.broadcasted_iota(jnp.int32, (total_rows, block), 1)
        return ids == column

    def score_step(step, carry):
        peak, total, positive = carry
        at = pl.ds(pl.multiple_of(step * block, block), block)
        product = (
            lax.dot_general(
                queries[...], keys[at, :], (((1,), (1,)), ((), ())),
                preferred_element_type=jnp.float32,
            )
            * factor
        )
        scores[:, at] = product
        new_peak = jnp.maximum(peak, jnp.max(product, axis=1, keepdims=True))
        total = total * jnp.exp(peak - new_peak) + jnp.sum(
            jnp.exp(product - new_peak), axis=1, keepdims=True
        )
        positive = positive + jnp.sum(
            jnp.where(is_positive(step), product, 0.0), axis=1, keepdims=True
        )
        return new_peak, total, positive

    zero = jnp.zeros((total_rows, 1), jnp.float32)
    peak, total, positive = lax.fori_loop(
        0, total_keys // block, score_step, (zero - 1e30, zero, zero)
    )
    for i in range(nz):
        at = slice(i * rows, (i + 1) * rows)
        stats[z, i, 0:1, :] = row_of(peak[at])
        stats[z, i, 1:2, :] = row_of(total[at])
        stats[z, i, 2:3, :] = row_of(positive[at])

    def stats_push(d, owner, target):
        at = stats.at[owner]
        return push(at, at, st_s.at[d], st_r.at[d], target, mp)

    for d in range(1, nz):
        start(stats_push(d, z, z_dev(d)))
    for d in range(1, nz):
        stats_push(d, lax.rem(z + nz - d, nz), me).wait_recv()

    top = stats[0, :, 0, :]
    for i in range(1, nz):
        top = jnp.maximum(top, stats[i, :, 0, :])
    whole = jnp.zeros_like(top)
    found = jnp.zeros_like(top)
    for i in range(nz):
        whole = whole + stats[i, :, 1, :] * jnp.exp(stats[i, :, 0, :] - top)
        found = found + stats[i, :, 2, :]
    log_rows = top + jnp.log(jnp.maximum(whole, 1e-30))
    losses = log_rows - found
    loss_line = jnp.zeros((1, LANES), jnp.float32)
    for i in range(nz):
        loss_line = loss_line + jnp.where(z == i, losses[i : i + 1, :], 0.0)
    loss_ref[...] = jnp.broadcast_to(loss_line, loss_ref.shape)
    log_total = jnp.concatenate(
        [column_of(log_rows[i : i + 1, :], 0, rows) for i in range(nz)], axis=0
    )

    @pl.loop(0, total_keys // block)
    def _(step):
        at = pl.ds(pl.multiple_of(step * block, block), block)
        probs[:, at] = (
            jnp.exp(scores[:, at] - log_total) - jnp.where(is_positive(step), 1.0, 0.0)
        ).astype(jnp.bfloat16)

    n_blocks = width // block

    def grad_push(d, c, source, owner, target):
        return push(
            partial.at[c, z_rows(owner), :], arrived.at[source, c],
            g_s.at[d, c], g_r.at[d, c], target, mp,
        )

    for c in range(n_blocks):
        partial[c] = jnp.dot(
            probs[...], keys[:, c * block : (c + 1) * block], preferred_element_type=jnp.float32
        ).astype(jnp.bfloat16)
        for d in range(1, nz):
            owner = lax.rem(z + d, nz)
            start(grad_push(d, c, z, owner, z_dev(d)))

    scaled = []
    inner = jnp.zeros((rows, 1), jnp.float32)
    for c in range(n_blocks):
        summed = partial[c, own_rows, :].astype(jnp.float32)
        for d in range(1, nz):
            source = lax.rem(z + nz - d, nz)
            grad_push(d, c, source, z, me).wait_recv()
            summed = summed + arrived[source, c].astype(jnp.float32)
        at = slice(c * block, (c + 1) * block)
        block_scaled = gain_ref[:, at] * (summed * (16.0 * factor))
        scaled.append(block_scaled)
        inner = inner + jnp.sum(block_scaled * hidden[:, at], axis=1, keepdims=True)
    inner = inverse_rms * inverse_rms * inverse_rms * inner / width
    hidden_grad = jnp.concatenate(
        [
            (inverse_rms * scaled[c] - hidden[:, c * block : (c + 1) * block] * inner).astype(
                jnp.bfloat16
            )
            for c in range(n_blocks)
        ],
        axis=1,
    )
    result = jnp.zeros((rows, width), jnp.float32)
    for m in range(n_mp):
        result = result + lax.dot_general(
            hidden_grad[:, m * part_width : (m + 1) * part_width], weights_in[m],
            (((1,), (1,)), ((), ())), preferred_element_type=jnp.float32,
        )
    grad_ref[...] = result.astype(jnp.bfloat16)
    for copy in sends:
        copy.wait_send()


def shards(n_queue, n_mp, speech, weight, norm_gain, queue_keys, new_keys, pointer, positives):
    rows, width = speech.shape
    key_count = queue_keys.shape[0]
    nz = n_queue // GROUP
    vmem = pl.BlockSpec(memory_space=pltpu.VMEM)
    anywhere = pl.BlockSpec(memory_space=pl.ANY)
    dma = pltpu.SemaphoreType.DMA
    bf16, f32 = jnp.bfloat16, jnp.float32
    line = jnp.broadcast_to(jnp.pad(positives, (0, LANES - rows))[None, :], (8, LANES))
    scratch = [
        pltpu.VMEM((GROUP * key_count, width), bf16),
        pltpu.VMEM((n_mp, width, width // n_mp), bf16),
        pltpu.VMEM((nz * rows, width), bf16),
        pltpu.VMEM((nz, 8, LANES), jnp.int32),
        pltpu.VMEM((nz * rows, GROUP * key_count), f32),
        pltpu.VMEM((nz * rows, GROUP * key_count), bf16),
        pltpu.VMEM((rows, width), f32),
        pltpu.VMEM((width // 256, nz * rows, 256), bf16),
        pltpu.VMEM((nz, width // 256, rows, 256), bf16),
        pltpu.VMEM((nz, nz, 8, LANES), f32),
        dma((2,)),
    ]
    scratch += [dma((n_mp, WEIGHT_CHUNKS))] * 10
    scratch += [dma((1,))] * 2 + [dma((KEY_CHUNKS,))] * 2 + [dma((n_mp, KEY_CHUNKS))] * 2
    scratch += [dma((KEY_CHUNKS,))] * 2 + [dma((n_mp, KEY_CHUNKS))] * 2
    scratch += [dma((nz,))] * 6 + [dma((nz, width // 256))] * 2
    loss, grad, queue_next = pl.pallas_call(
        functools.partial(step_kernel, n_queue, n_mp),
        out_shape=(
            jax.ShapeDtypeStruct((8, LANES), f32),
            jax.ShapeDtypeStruct((rows, width), bf16),
            jax.ShapeDtypeStruct((key_count, width), bf16),
        ),
        in_specs=[vmem, anywhere, vmem, anywhere, vmem, pl.BlockSpec(memory_space=pltpu.SMEM), vmem],
        out_specs=(vmem, vmem, vmem),
        scratch_shapes=scratch,
        compiler_params=pltpu.CompilerParams(
            collective_id=0, has_side_effects=True, vmem_limit_bytes=52 * 1024 * 1024
        ),
        name="contrast_step",
    )(speech, weight, norm_gain[None, :], queue_keys, new_keys, pointer, line)
    return loss[0, :rows], grad, queue_next


def solution(mesh):
    n_queue, n_mp = mesh.shape["queue"], mesh.shape["mp"]
    return jax.shard_map(
        functools.partial(shards, n_queue, n_mp),
        mesh=mesh,
        in_specs=(
            P(("queue", "mp"), None),
            P(None, "mp"),
            P(),
            P("queue", None),
            P(),
            P(),
            P(("queue", "mp")),
        ),
        out_specs=(P(("queue", "mp")), P(("queue", "mp"), None), P("queue", None)),
        check_vma=False,
    )
```

time: 304 us -> 87 us (0.29)
  waiting for transfers between devices: 123 us -> 0 us
  blocking collectives: 102 us -> 0 us
  Pallas kernels: 0 us -> 78.1 us
  matrix products: 29.2 us -> 0 us
  local copies, waits for them, and re-layouts: 23.5 us -> 7.36 us
  between operations: 15.2 us -> 1.29 us
  other arithmetic: 9.69 us -> 0 us
    pallas_call x0 -> x1, Pallas kernels: none -> 78.1 us  [shards(): pl.pallas_call(functools.partial(step_kernel, n_queue, n_mp), out_shape=(...]
    all_gather x2 -> x0, waiting for transfers between devices: 68.2 us -> none  [the longest x1 37.4 us: shards(): full_weight = lax.all_gather(weight, 'mp', axis=1, tiled=True)]
    psum x1 -> x0, blocking collectives: 57.6 us -> none  [shards(): lax.psum((row_total * jnp.exp(row_peak - global_peak), row_positive), 'qu...]
    reduce_scatter x1 -> x0, waiting for transfers between devices: 54.3 us -> none  [shards(): lax.psum_scatter(weighted_rows(scores, log_total, columns, queue_keys).as...]
    pmax x1 -> x0, blocking collectives: 32 us -> none  [shards(): global_peak = lax.pmax(row_peak, 'queue')]
    dot_general x8 -> x0, matrix products: 29.2 us -> none  [the longest x3 12 us: weight_block(): return jnp.dot(weights, key_rows, preferred_element_type=jnp.float32)]
    unnamed x1 -> x0, blocking collectives: 12.3 us -> none
    dynamic_update_slice x9 -> x0, local copies, waits for them, and re-layouts: 11.8 us -> none  [score_rows(): lax.map(score_block, (all_queries.reshape(block_count, block_rows, -1), c...]
  transfers between devices with their start and end apart: 3 -> 0, of which waited for: 3 -> 0; matrix products, arithmetic and copies ran while one was open for 3% -> 0% of each run, Pallas kernels for 0% -> 0%
where the time goes in v1:
time: 87 us; the launch traced here: 86.7 us
  Pallas kernels  78.1 us (90%)
  local copies, waits for them, and re-layouts  7.36 us (8%)
  between operations  1.29 us (1%)
    pallas_call x1, Pallas kernels, shards(): pl.pallas_call(functools.partial(step_kernel, n_queue, n_mp), out_shape=(...  78.1 us
    unnamed x8, local copies, waits for them, and re-layouts  6.18 us

profile of v1, /device:TPU:0, one launch (start us, length us, event | category | flops | bytes accessed | tf_op | source)
XLA Modules:
  0.0 86.7 jit_solution(12610907937625042056)
XLA Ops:
  1.3 0.7 pad.4
  1.9 0.0 copy-start
  1.9 1.2 %copy-done = bf16[1024,512]{1,0:T(8,128)(2,1)S(1)} copy-done((bf16[1024,512]{1,0:T(8,128)(2,1)S(1)}, bf16[1024,512]{1,0:T(8,128)(2,1)}, u32[]{:S(2)}) %copy-start) | copy-done | bytes 1048600
  3.2 0.0 copy-start.1
  3.2 0.9 %copy-done.1 = bf16[96,1024]{1,0:T(8,128)(2,1)S(1)} copy-done((bf16[96,1024]{1,0:T(8,128)(2,1)S(1)}, bf16[96,1024]{1,0:T(8,128)(2,1)}, u32[]{:S(2)}) %copy-start.1) | copy-done | bytes 196632
  4.1 0.0 copy-start.2
  4.1 0.7 copy-done.2
  4.8 78.1 %contrast_step.1 = (f32[8,128]{1,0:T(8,128)S(1)}, bf16[96,1024]{1,0:T(8,128)(2,1)S(1)}, bf16[768,1024]{1,0:T(8,128)(2,1)}) custom-call(bf16[96,1024]{1,0:T(8,128)(2,1)S(1)} %copy-done.1, bf16[1024,512]{1,0:T(8,128)(2,1)S(1)} %copy-done, f32[1,1024]{1,0:T(1,128)S(1)} %bitcast.3, bf16[768,1024]{1,0:T(8,128)(2,1)} %keys_ref.1, bf16[768,1024]{1,0:T(8,128)(2,1)} %new_ref.1, ...), custom_call_target="tpu_custom_call" | custom-call | tf_op jit(solution)/shard_map/contrast_step/pallas_call | solution.py:391
  82.8 0.5 slice_bitcast_fusion
  83.4 0.7 copy.13
  84.0 2.7 %copy.14 = bf16[768,1024]{1,0:T(8,128)(2,1)} copy(bf16[768,1024]{1,0:T(8,128)(2,1)} %get-tuple-element.14) | data formatting | bytes 3145728
  (1 shorter events, 0.0 us)
Async XLA Ops:
  1.9 1.2 %copy-start = (bf16[1024,512]{1,0:T(8,128)(2,1)S(1)}, bf16[1024,512]{1,0:T(8,128)(2,1)}, u32[]{:S(2)}) copy-start(bf16[1024,512]{1,0:T(8,128)(2,1)} %weight_ref.1) | copy-start | bytes 3145732
  3.2 0.9 %copy-start.1 = (bf16[96,1024]{1,0:T(8,128)(2,1)S(1)}, bf16[96,1024]{1,0:T(8,128)(2,1)}, u32[]{:S(2)}) copy-start(bf16[96,1024]{1,0:T(8,128)(2,1)} %speech_ref.1) | copy-start | bytes 589828
  4.1 0.7 copy-start.2
